TPU v7x, 32 devices: a whole 2x2x4 slice. The times are simulated.
32 devices in a mesh: section: 16 (over z, y, x), tensor: 2 (over core).
Axes of the slice: x: 2, y: 2, z: 4, core: 2. Of those that a mesh axis runs over, the one named last changes fastest.
Arguments:
- section_norm_gain: float32 [16, 4096], P('section'), may hold values from 0.5 to 1.5
- query_weight_matrix: bfloat16 [16, 4096, 4096], P('section', None, 'tensor'), may hold values from -2 to 2
- key_weight_matrix: bfloat16 [16, 4096, 1024], P('section', None, 'tensor'), may hold values from -2 to 2
- value_weight_matrix: bfloat16 [16, 4096, 1024], P('section', None, 'tensor'), may hold values from -0.09375 to 0.09375
- output_weight_matrix: bfloat16 [16, 4096, 4096], P('section', 'tensor'), may hold values from -0.09375 to 0.09375
- adapter_down_weight: bfloat16 [16, 2, 8, 4096], P('section'), may hold values from -0.09375 to 0.09375
- query_up_weight: bfloat16 [16, 8, 4096], P('section', None, 'tensor'), may hold values from -2 to 2
- value_up_weight: bfloat16 [16, 8, 1024], P('section', None, 'tensor'), may hold values from -2 to 2
- arriving: bfloat16 [16, 128, 4096], P('section', None, 'tensor'), may hold values from -6 to 6
- entering: bfloat16 [1, 128, 4096], P(None, None, 'tensor'), may hold values from -6 to 6
- returning: bfloat16 [16, 128, 4096], P('section', None, 'tensor'), may hold values from -6 to 6
- loss_head_gradient: bfloat16 [1, 128, 4096], P(None, None, 'tensor'), may hold values from -6 to 6
- parked: bfloat16 [16, 2, 128, 4096], P('section', None, None, 'tensor'), may hold values from -6 to 6
- forward_document_ids: int32 [17, 128], replicated, may hold values from 0 to 3, never falling along the last dimension, each value on 1 to 64 neighbouring positions
- backward_document_ids: int32 [17, 128], replicated, may hold values from 0 to 3, never falling along the last dimension, each value on 1 to 64 neighbouring positions
Outputs:
- departing: bfloat16 [16, 128, 4096], P('section', None, 'tensor')
- returned: bfloat16 [16, 128, 4096], P('section', None, 'tensor')
- parked_out: bfloat16 [16, 2, 128, 4096], P('section', None, None, 'tensor')
- grad_down: float32 [16, 2, 8, 4096], P('section', None, None, 'tensor')
- grad_up_query: float32 [16, 8, 4096], P('section', None, 'tensor')
- grad_up_value: float32 [16, 8, 1024], P('section', None, 'tensor')
Inputs may be any that keep to these rules, and one draw needn't show every extreme that they name: `forward_document_ids`: document ids never fall along a row; each of the 4 documents of a micro-batch holds 1 to 64 positions. `backward_document_ids`: document ids never fall along a row; each of the 4 documents of a micro-batch holds 1 to 64 positions.
All inputs are finite; a program needn't handle non-finite values.
Results may differ from a plain program's by a relative error of at most 0.024.
The roundings to bfloat16 on the way count: a program that leaves them out, or rounds other values in their place, can miss the bound.
Values may be sent and summed in bfloat16 or wider, within the bound.
A program may use at most 192 MiB of HBM per device.

v0:
```python
import math

import jax
import jax.numpy as jnp
from jax import lax
from jax.sharding import PartitionSpec as P

HEAD = 128


eps = 1e-05
rope_base = 500000.0
mask_fill = -1e30


def passed_along(block, axis, distance):
    devices = range(lax.axis_size(axis))
    route = [(i - distance, i) for i in devices if i - distance in devices]
    return lax.ppermute(block, axis, route)


def partner(value, axis, apart):
    mask = 2**apart
    pairs = [(source, source ^ mask) for source in range(lax.axis_size(axis))]
    return lax.ppermute(value, axis, pairs)


def rope_tables(row_count, head_size):
    half_size = head_size // 2
    exponent = jnp.arange(half_size, dtype=jnp.float32) * (2.0 / head_size)
    frequency = jnp.exp(-exponent * math.log(rope_base))
    angles = jnp.arange(row_count, dtype=jnp.float32)[:, None] * frequency[None, :]
    return (jnp.cos(angles), jnp.sin(angles))


def rotate(value_rows_block, cosine_lookup, sine_lookup, direction):
    half_size = value_rows_block.shape[-1] // 2
    first_half = value_rows_block[..., :half_size]
    second = value_rows_block[..., half_size:]
    target_shape = (cosine_lookup.shape[0],) + (1,) * (value_rows_block.ndim - 2) + (half_size,)
    cosines = cosine_lookup.reshape(target_shape)
    sines = sine_lookup.reshape(target_shape) * direction
    return jnp.concatenate(
        [first_half * cosines - second * sines, second * cosines + first_half * sines], axis=-1
    )


def apply_projection(
    section_inputs,
    norm_gain_vector,
    query_weight_matrix,
    key_weight_matrix,
    value_weight_matrix,
    adapter_down_weight,
    query_up_weight,
    value_up_weight,
    cosine_lookup,
    sine_lookup,
):
    adapter_rank_size = query_up_weight.shape[0]
    head_size = cosine_lookup.shape[1] * 2
    row_count = section_inputs.shape[0]
    groups = key_weight_matrix.shape[1] // head_size
    per_group = query_weight_matrix.shape[1] // head_size // groups
    inputs_single_float = section_inputs.astype(jnp.float32)
    inverse_root_mean = lax.rsqrt(
        jnp.mean(inputs_single_float * inputs_single_float, axis=1, keepdims=True) + eps
    )
    normalized_input = (inputs_single_float * inverse_root_mean * norm_gain_vector[None, :]).astype(
        jnp.bfloat16
    )
    flattened_down = adapter_down_weight.reshape(
        2 * adapter_rank_size, adapter_down_weight.shape[-1]
    )
    low_rank_output = lax.dot_general(
        normalized_input,
        flattened_down,
        (((1,), (1,)), ((), ())),
        preferred_element_type=jnp.float32,
    ).astype(jnp.bfloat16)
    query_rows_block = jnp.dot(
        normalized_input, query_weight_matrix, preferred_element_type=jnp.float32
    ) + jnp.dot(
        low_rank_output[:, :adapter_rank_size], query_up_weight, preferred_element_type=jnp.float32
    )
    key_row_block = jnp.dot(normalized_input, key_weight_matrix, preferred_element_type=jnp.float32)
    value_rows_block = jnp.dot(
        normalized_input, value_weight_matrix, preferred_element_type=jnp.float32
    ) + jnp.dot(
        low_rank_output[:, adapter_rank_size:], value_up_weight, preferred_element_type=jnp.float32
    )
    query_rows_block = rotate(
        query_rows_block.reshape(row_count, groups, per_group, head_size),
        cosine_lookup,
        sine_lookup,
        1.0,
    ).astype(jnp.bfloat16)
    key_row_block = rotate(
        key_row_block.reshape(row_count, groups, head_size), cosine_lookup, sine_lookup, 1.0
    ).astype(jnp.bfloat16)
    value_rows_block = value_rows_block.reshape(row_count, groups, head_size).astype(jnp.bfloat16)
    return (
        inputs_single_float,
        inverse_root_mean,
        normalized_input,
        low_rank_output,
        query_rows_block,
        key_row_block,
        value_rows_block,
    )


def allowed_pairs(document_list):
    positions = jnp.arange(document_list.shape[0], dtype=jnp.int32)
    return (positions[None, :] <= positions[:, None]) & (
        document_list[:, None] == document_list[None, :]
    )


def attend(query_rows_block, key_row_block, value_rows_block, allowed):
    inverse = 1.0 / math.sqrt(query_rows_block.shape[-1])
    scores = (
        jnp.einsum(
            "qgd,kd->gqk", query_rows_block, key_row_block, preferred_element_type=jnp.float32
        )
        * inverse
    )
    scores = jnp.where(allowed[None, :, :], scores, mask_fill)
    row_max = jnp.max(scores, axis=2, keepdims=True)
    weights = jnp.exp(scores - row_max)
    probabilities = weights / jnp.sum(weights, axis=2, keepdims=True)
    rounded = probabilities.astype(jnp.bfloat16)
    context = jnp.einsum(
        "gqk,kd->qgd", rounded, value_rows_block, preferred_element_type=jnp.float32
    )
    return (probabilities, rounded, context)


def attend_back(
    query_rows_block, key_row_block, value_rows_block, probabilities, rounded, d_context
):
    inverse = 1.0 / math.sqrt(query_rows_block.shape[-1])
    d_probs = jnp.einsum(
        "qgd,kd->gqk", d_context, value_rows_block, preferred_element_type=jnp.float32
    )
    d_values = jnp.einsum("gqk,qgd->kd", rounded, d_context, preferred_element_type=jnp.float32)
    d_score = (
        probabilities
        * (d_probs - jnp.sum(d_probs * probabilities, axis=2, keepdims=True))
        * inverse
    )
    score_grad = d_score.astype(jnp.bfloat16)
    d_queries = jnp.einsum(
        "gqk,kd->qgd", score_grad, key_row_block, preferred_element_type=jnp.float32
    )
    d_keys = jnp.einsum(
        "gqk,qgd->kd", score_grad, query_rows_block, preferred_element_type=jnp.float32
    )
    return (d_queries, d_keys, d_values)


def section_loss_term(
    section_inputs,
    norm_gain_vector,
    query_weight_matrix,
    key_weight_matrix,
    value_weight_matrix,
    output_weight_matrix,
    adapter_down_weight,
    query_up_weight,
    value_up_weight,
    document_list,
    cosine_lookup,
    sine_lookup,
):
    partial_pieces = apply_projection(
        section_inputs,
        norm_gain_vector,
        query_weight_matrix,
        key_weight_matrix,
        value_weight_matrix,
        adapter_down_weight,
        query_up_weight,
        value_up_weight,
        cosine_lookup,
        sine_lookup,
    )
    allowed = allowed_pairs(document_list)
    probabilities, rounded, context = jax.vmap(attend, in_axes=(1, 1, 1, None), out_axes=(0, 0, 1))(
        partial_pieces[4], partial_pieces[5], partial_pieces[6], allowed
    )
    context = context.reshape(section_inputs.shape[0], -1).astype(jnp.bfloat16)
    return jnp.dot(context, output_weight_matrix, preferred_element_type=jnp.float32)


def section_backward_pass(
    section_inputs,
    incoming_cotangent,
    norm_gain_vector,
    query_weight_matrix,
    key_weight_matrix,
    value_weight_matrix,
    output_weight_matrix,
    adapter_down_weight,
    query_up_weight,
    value_up_weight,
    document_list,
    cosine_lookup,
    sine_lookup,
):
    (
        inputs_single_float,
        inverse_root_mean,
        normalized_input,
        low_rank_output,
        query_rows_block,
        key_row_block,
        value_rows_block,
    ) = apply_projection(
        section_inputs,
        norm_gain_vector,
        query_weight_matrix,
        key_weight_matrix,
        value_weight_matrix,
        adapter_down_weight,
        query_up_weight,
        value_up_weight,
        cosine_lookup,
        sine_lookup,
    )
    adapter_rank_size = query_up_weight.shape[0]
    row_count = section_inputs.shape[0]
    allowed = allowed_pairs(document_list)
    probabilities, rounded, context = jax.vmap(attend, in_axes=(1, 1, 1, None), out_axes=(0, 0, 1))(
        query_rows_block, key_row_block, value_rows_block, allowed
    )
    last_dims = (((1,), (1,)), ((), ()))
    leading_dimensions = (((0,), (0,)), ((), ()))
    d_context = (
        lax.dot_general(
            incoming_cotangent, output_weight_matrix, last_dims, preferred_element_type=jnp.float32
        )
        .astype(jnp.bfloat16)
        .reshape(query_rows_block.shape)
    )
    d_queries, d_keys, d_values = jax.vmap(
        attend_back, in_axes=(1, 1, 1, 0, 0, 1), out_axes=(1, 1, 1)
    )(query_rows_block, key_row_block, value_rows_block, probabilities, rounded, d_context)
    query_grad = (
        rotate(d_queries, cosine_lookup, sine_lookup, -1.0)
        .astype(jnp.bfloat16)
        .reshape(row_count, -1)
    )
    key_grad = (
        rotate(d_keys, cosine_lookup, sine_lookup, -1.0).astype(jnp.bfloat16).reshape(row_count, -1)
    )
    value_grad = d_values.astype(jnp.bfloat16).reshape(row_count, -1)
    low_rank_gradient = jnp.concatenate(
        [
            lax.dot_general(
                query_grad, query_up_weight, last_dims, preferred_element_type=jnp.float32
            ),
            lax.dot_general(
                value_grad, value_up_weight, last_dims, preferred_element_type=jnp.float32
            ),
        ],
        axis=1,
    ).astype(jnp.bfloat16)
    flattened_down = adapter_down_weight.reshape(
        2 * adapter_rank_size, adapter_down_weight.shape[-1]
    )
    d_normed = lax.dot_general(
        query_grad, query_weight_matrix, last_dims, preferred_element_type=jnp.float32
    )
    d_normed = d_normed + lax.dot_general(
        key_grad, key_weight_matrix, last_dims, preferred_element_type=jnp.float32
    )
    d_normed = d_normed + lax.dot_general(
        value_grad, value_weight_matrix, last_dims, preferred_element_type=jnp.float32
    )
    d_normed = d_normed + jnp.dot(
        low_rank_gradient, flattened_down, preferred_element_type=jnp.float32
    )
    weighted = d_normed * norm_gain_vector[None, :]
    d_inputs = inverse_root_mean * weighted - inputs_single_float * inverse_root_mean**3 * jnp.mean(
        inputs_single_float * weighted, axis=1, keepdims=True
    )
    down_gradient = lax.dot_general(
        low_rank_gradient, normalized_input, leading_dimensions, preferred_element_type=jnp.float32
    ).reshape(adapter_down_weight.shape)
    up_query_grad = lax.dot_general(
        low_rank_output[:, :adapter_rank_size],
        query_grad,
        leading_dimensions,
        preferred_element_type=jnp.float32,
    )
    up_value_grad = lax.dot_general(
        low_rank_output[:, adapter_rank_size:],
        value_grad,
        leading_dimensions,
        preferred_element_type=jnp.float32,
    )
    return (d_inputs, down_gradient, up_query_grad, up_value_grad)


def per_device(
    section_norm_gain,
    query_weight_matrix,
    key_weight_matrix,
    value_weight_matrix,
    output_weight_matrix,
    adapter_down_weight,
    query_up_weight,
    value_up_weight,
    arriving,
    entering,
    returning,
    loss_head_gradient,
    parked,
    forward_document_ids,
    backward_document_ids,
):
    section_count = lax.axis_size("section")
    section_index = lax.axis_index("section")
    tensor_index = lax.axis_index("tensor")
    partner_bit = section_count.bit_length() - 2
    tick_count = parked.shape[1]
    row_count = arriving.shape[1]
    feature_share = arriving.shape[2]
    cosine_lookup, sine_lookup = rope_tables(row_count, HEAD)
    norm_gain_vector = section_norm_gain[0]
    query_proj = query_weight_matrix[0]
    key_proj = key_weight_matrix[0]
    value_proj = value_weight_matrix[0]
    out_proj = output_weight_matrix[0]
    down_projected = adapter_down_weight[0]
    up_queries = query_up_weight[0]
    up_values = value_up_weight[0]
    first_input, entering_rows, first_cotangent, head_rows = (
        lax.all_gather(arriving[0], "tensor", axis=1, tiled=True),
        lax.all_gather(entering.reshape(-1, feature_share), "tensor", axis=1, tiled=True),
        lax.all_gather(returning[0], "tensor", axis=1, tiled=True),
        lax.all_gather(loss_head_gradient.reshape(-1, feature_share), "tensor", axis=1, tiled=True),
    )
    entering_all = entering_rows.reshape(tick_count - 1, row_count, -1)
    head_all = head_rows.reshape(tick_count - 1, row_count, -1)

    def narrow(held_rows):
        return lax.dynamic_slice_in_dim(held_rows, tensor_index * feature_share, feature_share, 1)

    def combine(base_rows, partial_value):
        return (
            base_rows.astype(jnp.float32)
            + lax.psum(partial_value.astype(jnp.bfloat16), "tensor").astype(jnp.float32)
        ).astype(jnp.bfloat16)

    held_rows = first_input
    result_rows = first_input
    stashed = []
    for moment in range(tick_count):
        if moment > 0:
            held_rows = jnp.where(
                section_index == 0,
                entering_all[moment - 1],
                passed_along(result_rows, "section", 1),
            )
        stashed.append(narrow(held_rows))
        document_list = lax.dynamic_index_in_dim(
            forward_document_ids, moment - section_index + section_count - 1, 0, keepdims=False
        )
        partial_value = section_loss_term(
            held_rows,
            norm_gain_vector,
            query_proj,
            key_proj,
            value_proj,
            out_proj,
            down_projected,
            up_queries,
            up_values,
            document_list,
            cosine_lookup,
            sine_lookup,
        )
        result_rows = combine(held_rows, partial_value)
    departing = narrow(result_rows)
    parked_new = jnp.stack(
        [partner(stored_rows, "section", partner_bit) for stored_rows in stashed], axis=0
    )
    cotangent_held = first_cotangent
    gradient_held = first_cotangent
    down_gradient_sum = jnp.zeros(down_projected.shape, jnp.float32)
    query_total = jnp.zeros(up_queries.shape, jnp.float32)
    value_total = jnp.zeros(up_values.shape, jnp.float32)
    for moment in range(tick_count):
        if moment > 0:
            cotangent_held = jnp.where(
                section_index == section_count - 1,
                head_all[moment - 1],
                passed_along(gradient_held, "section", -1),
            )
        stored_full = lax.all_gather(
            partner(parked[0, moment], "section", partner_bit), "tensor", axis=1, tiled=True
        )
        document_list = lax.dynamic_index_in_dim(
            backward_document_ids, section_index + moment, 0, keepdims=False
        )
        partial_value, down_gradient, up_query_grad, up_value_grad = section_backward_pass(
            stored_full,
            cotangent_held,
            norm_gain_vector,
            query_proj,
            key_proj,
            value_proj,
            out_proj,
            down_projected,
            up_queries,
            up_values,
            document_list,
            cosine_lookup,
            sine_lookup,
        )
        gradient_held = combine(cotangent_held, partial_value)
        down_gradient_sum = down_gradient_sum + down_gradient
        query_total = query_total + up_query_grad
        value_total = value_total + up_value_grad
    returned = narrow(gradient_held)
    down_share = lax.psum_scatter(
        down_gradient_sum.astype(jnp.bfloat16), "tensor", scatter_dimension=2, tiled=True
    ).astype(jnp.float32)
    return (
        departing[None],
        returned[None],
        parked_new[None],
        down_share[None],
        query_total[None],
        value_total[None],
    )


def solution(mesh):
    placed = (
        P("section", None),
        P("section", None, "tensor"),
        P("section", None, "tensor"),
        P("section", None, "tensor"),
        P("section", "tensor", None),
        P("section", None, None, None),
        P("section", None, "tensor"),
        P("section", None, "tensor"),
        P("section", None, "tensor"),
        P(None, None, "tensor"),
        P("section", None, "tensor"),
        P(None, None, "tensor"),
        P("section", None, None, "tensor"),
        P(),
        P(),
    )
    return jax.shard_map(
        per_device,
        mesh=mesh,
        in_specs=placed,
        out_specs=(
            P("section", None, "tensor"),
            P("section", None, "tensor"),
            P("section", None, None, "tensor"),
            P("section", None, None, "tensor"),
            P("section", None, "tensor"),
            P("section", None, "tensor"),
        ),
        check_vma=False,
    )
```

profile of v0, /device:TPU:0, one launch (start us, length us, event | category | flops | bytes accessed | tf_op | source)
XLA Modules:
  0.0 450.5 jit_solution(11605701283822398067)
XLA Ops:
  10.0 4.1 collective-permute-start.1
  14.1 23.2 %collective-permute-done.1 = bf16[128,2048]{1,0:T(8,128)(2,1)S(1)} collective-permute-done((bf16[128,2048]{1,0:T(8,128)(2,1)S(1)}, bf16[128,2048]{1,0:T(8,128)(2,1)S(1)}, u32[]{:S(2)}, u32[]{:S(2)}) %collective-permute-start.1) | collective-permute-done | bytes 524320 | tf_op jit(solution)/shard_map/ppermute | solution.py:25
  38.7 6.4 %copy.138 = bf16[512,4096]{1,0:T(8,128)(2,1)} copy(bf16[512,4096]{0,1:T(8,128)(2,1)} %bitcast.370) | data formatting | bytes 8388608 | tf_op jit(solution)/shard_map/dot_general | solution.py:86
  48.7 14.7 %collective-permute-done.3 = bf16[128,2048]{1,0:T(8,128)(2,1)S(1)} collective-permute-done((bf16[128,2048]{1,0:T(8,128)(2,1)S(1)}, bf16[128,2048]{1,0:T(8,128)(2,1)S(1)}, u32[]{:S(2)}, u32[]{:S(2)}) %collective-permute-start.3) | collective-permute-done | bytes 524320 | tf_op jit(solution)/shard_map/ppermute | solution.py:25
  67.7 8.7 %fusion.24 = f32[128,2048]{1,0:T(8,128)S(1)} fusion(bf16[1,4096,2048]{2,1,0:T(8,128)(2,1)} %param.16, bf16[1,128,4096]{2,1,0:T(8,128)(2,1)S(1)} %copy-done.6, f32[4096]{0:T(1024)S(1)} %bitcast.389, f32[128]{0:T(128)S(1)} %add_rsqrt_fusion.3), kind=kOutput, calls=%fused_computation.24 | convolution fusion | flops 2149580800 | bytes 18891264 | tf_op jit(solution)/shard_map/dot_general | solution.py:81
  79.4 11.8 %fusion.54 = bf16[128,2048]{1,0:T(8,128)(2,1)S(1)} fusion(bf16[1,2048,4096]{2,1,0:T(8,128)(2,1)} %param.19, bf16[1,128,4096]{2,1,0:T(8,128)(2,1)} %all-gather.21.cloned.1.call-done), kind=kOutput, calls=%fused_computation.66 | convolution fusion | flops 2147745792 | bytes 18350080 | tf_op jit(solution)/shard_map/dot_general | solution.py:240
  92.2 3.0 fusion.46
  96.1 4.2 fusion.133
  105.4 8.5 %fusion.48 = f32[128,2048]{1,0:T(8,128)S(1)} fusion(f32[128,2048]{1,0:T(8,128)S(1)} %fusion.191, bf16[1,4096,2048]{2,1,0:T(8,128)(2,1)} %param.16, bf16[128,4096]{1,0:T(8,128)(2,1)S(1)} %copy-done.2, f32[128]{0:T(128)S(1)} %get-tuple-element.61, f32[4096]{0:T(1024)S(1)} %bitcast.393), kind=kOutput, calls=%fused_computation.64 | convolution fusion | flops 2149842944 | bytes 19939840 | tf_op jit(solution)/shard_map/dot_general | solution.py:81
  115.2 2.3 fusion.301
  118.9 2.4 copy.144
  121.3 3.6 fusion.118
  126.5 3.6 fusion.128
  132.3 2.3 subtract_convert_fusion.1
  134.6 3.5 fusion.306
  139.7 3.8 convolution_bitcast_fusion.7
  143.5 2.8 convolution_bitcast_fusion.2
  148.2 23.3 %fusion.18 = f32[128,4096]{1,0:T(8,128)} fusion(bf16[128,2048]{0,1:T(8,128)(2,1)S(1)} %bitcast.374, bf16[1,4096,2048]{2,1,0:T(8,128)(2,1)} %param.16), kind=kOutput, calls=%fused_computation.18 | convolution fusion | flops 2147483648 | bytes 19398656 | tf_op jit(solution)/shard_map/dot_general | solution.py:272
  173.0 4.5 convolution_add_fusion.5
  177.5 2.8 convolution_add_fusion.4
  180.3 2.1 fusion.303
  182.4 2.0 convolution_convert_fusion.1
  184.5 9.2 %fusion.28 = bf16[128,4096]{1,0:T(8,128)(2,1)} fusion(bf16[128,2048]{0,1:T(8,128)(2,1)S(1)} %bitcast.415, bf16[1,2048,4096]{2,1,0:T(8,128)(2,1)} %param.19), kind=kOutput, calls=%fused_computation.34 | convolution fusion | flops 2148007936 | bytes 18350080 | tf_op jit(solution)/shard_map/dot_general | solution.py:193
  199.7 2.0 convolution_convert_fusion.2
  203.9 9.2 %fusion.51 = f32[128,2048]{1,0:T(8,128)} fusion(f32[128,2048]{1,0:T(8,128)S(1)} %fusion.188, bf16[1,4096,2048]{2,1,0:T(8,128)(2,1)} %param.16, bf16[128,4096]{1,0:T(8,128)(2,1)S(1)} %copy-done.1, f32[128]{0:T(128)S(1)} %get-tuple-element.59, f32[4096]{0:T(1024)S(1)} %bitcast.398), kind=kOutput, calls=%fused_computation.65 | convolution fusion | flops 2149842944 | bytes 19939840 | tf_op jit(solution)/shard_map/dot_general | solution.py:81
  213.1 2.6 copy.85
  215.7 2.3 fusion.299
  218.0 4.4 fusion.126
  223.8 2.5 fusion.64
  226.3 4.0 collective-permute-start
  231.5 2.5 copy.145
  234.0 2.4 copy.146
  238.0 2.5 add_convert_fusion
  242.2 30.7 %collective-permute-done = bf16[128,4096]{1,0:T(8,128)(2,1)} collective-permute-done((bf16[128,4096]{1,0:T(8,128)(2,1)}, bf16[128,4096]{1,0:T(8,128)(2,1)}, u32[]{:S(2)}, u32[]{:S(2)}) %collective-permute-start) | collective-permute-done | bytes 1048608 | tf_op jit(solution)/shard_map/ppermute | solution.py:19
  274.6 8.1 %fusion.22 = f32[128,2048]{1,0:T(8,128)S(1)} fusion(bf16[1,4096,2048]{2,1,0:T(8,128)(2,1)} %param.16, f32[128]{0:T(128)S(1)} %add_rsqrt_fusion.2, bf16[128,4096]{1,0:T(8,128)(2,1)S(1)} %get-tuple-element.11, f32[4096]{0:T(1024)S(1)} %bitcast.402), kind=kOutput, calls=%fused_computation.22 | convolution fusion | flops 2149580800 | bytes 18891264 | tf_op jit(solution)/shard_map/dot_general | solution.py:81
  285.1 2.6 copy.63
  287.7 2.3 fusion.300
  289.9 2.4 copy.141
  292.3 2.4 copy.142
  294.7 4.2 fusion.131
  298.9 2.6 bitcast_select_fusion
  301.5 12.5 %fusion.57 = bf16[128,2048]{1,0:T(8,128)(2,1)} fusion(bf16[128,4096]{1,0:T(8,128)(2,1)} %bitcast_select_fusion, bf16[1,2048,4096]{2,1,0:T(8,128)(2,1)} %param.19), kind=kOutput, calls=%fused_computation.67 | convolution fusion | flops 2147745792 | bytes 18350080 | tf_op jit(solution)/shard_map/dot_general | solution.py:240
  314.1 2.0 copy.148
  316.1 2.0 subtract_convert_fusion.5
  318.1 2.5 convolution_bitcast_fusion.1
  320.6 3.3 subtract_convert_fusion
  324.0 3.5 fusion.310
  327.4 2.3 fusion.114
  329.8 3.8 convolution_bitcast_fusion
  333.6 4.3 convolution_bitcast_fusion.5
  338.0 2.0 multiply_subtract_fusion
  341.1 2.0 copy.93
  344.3 13.1 %fusion.14 = f32[128,4096]{1,0:T(8,128)} fusion(bf16[128,2048]{0,1:T(8,128)(2,1)} %bitcast.372, bf16[1,4096,2048]{2,1,0:T(8,128)(2,1)} %param.16), kind=kOutput, calls=%fused_computation.14 | convolution fusion | flops 2147483648 | bytes 19398656 | tf_op jit(solution)/shard_map/dot_general | solution.py:272
  359.4 2.0 fusion.35
  362.6 4.5 convolution_add_fusion.2
  375.6 2.9 convolution_convert_fusion
  378.5 3.2 fusion.77
  381.7 9.1 %fusion.31 = bf16[128,4096]{1,0:T(8,128)(2,1)} fusion(bf16[128,2048]{0,1:T(8,128)(2,1)S(1)} %bitcast.414, bf16[1,2048,4096]{2,1,0:T(8,128)(2,1)} %param.19), kind=kOutput, calls=%fused_computation.35 | convolution fusion | flops 2148007936 | bytes 18350080 | tf_op jit(solution)/shard_map/dot_general | solution.py:193
  394.9 2.6 collective-permute-start.5
  400.6 28.3 %collective-permute-done.4 = bf16[128,2048]{1,0:T(8,128)(2,1)} collective-permute-done((bf16[128,2048]{1,0:T(8,128)(2,1)}, bf16[128,2048]{1,0:T(8,128)(2,1)}, u32[]{:S(2)}, u32[]{:S(2)}) %collective-permute-start.4) | collective-permute-done | bytes 524320 | tf_op jit(solution)/shard_map/ppermute | solution.py:25
  428.9 8.8 %collective-permute-done.5 = bf16[128,2048]{1,0:T(8,128)(2,1)} collective-permute-done((bf16[128,2048]{1,0:T(8,128)(2,1)}, bf16[128,2048]{1,0:T(8,128)(2,1)}, u32[]{:S(2)}, u32[]{:S(2)}) %collective-permute-start.5) | collective-permute-done | bytes 524320 | tf_op jit(solution)/shard_map/ppermute | solution.py:25
  437.6 2.3 maximum_bitcast_fusion
  439.9 2.0 fusion.145
  441.9 1.9 fusion.146
  (248 shorter events, 72.5 us)
Async XLA Ops:
  7.2 58.8 %copy-start = (bf16[1,2,8,4096]{3,2,1,0:T(8,128)(2,1)S(1)}, bf16[1,2,8,4096]{3,2,1,0:T(8,128)(2,1)}, u32[]{:S(2)}) copy-start(bf16[1,2,8,4096]{3,2,1,0:T(8,128)(2,1)} %param.20) | copy-start | bytes 393220
  7.2 57.2 %all-gather.17.cloned.1.call-start = ((), (), s32[]{:S(2)}) async-start(), calls=%async_computation.5 | async-start | bytes 1572864 | tf_op jit(solution)/shard_map/all_gather | solution.py:340
  7.9 71.4 %all-gather.21.cloned.1.call-start = ((), (), s32[]{:S(2)}) async-start(), calls=%async_computation.7 | async-start | bytes 1572864 | tf_op jit(solution)/shard_map/all_gather | solution.py:342
  8.7 91.7 %all-gather.11.cloned.1.call-start = ((), (), s32[]{:S(2)}) async-start(), calls=%async_computation.1 | async-start | bytes 1572864 | tf_op jit(solution)/shard_map/all_gather | solution.py:402
  10.0 27.3 %collective-permute-start.1 = (bf16[128,2048]{1,0:T(8,128)(2,1)S(1)}, bf16[128,2048]{1,0:T(8,128)(2,1)S(1)}, u32[]{:S(2)}, u32[]{:S(2)}) collective-permute-start(bf16[128,2048]{1,0:T(8,128)(2,1)S(1)} %get-tuple-element.27), channel_id=1, source_target_pairs={{0,16},{2,18},{4,20},{6,22},{8,24},{10,26},{12,28},{14,30},{16,0},... | collective-permute-start | bytes 1572872 | tf_op jit(solution)/shard_map/ppermute | solution.py:25
  38.1 159.5 %all-gather.13.cloned.1.call-start = ((), (), s32[]{:S(2)}) async-start(), calls=%async_computation.2 | async-start | bytes 1572864 | tf_op jit(solution)/shard_map/all_gather | solution.py:402
  38.1 25.3 %collective-permute-start.3 = (bf16[128,2048]{1,0:T(8,128)(2,1)S(1)}, bf16[128,2048]{1,0:T(8,128)(2,1)S(1)}, u32[]{:S(2)}, u32[]{:S(2)}) collective-permute-start(bf16[128,2048]{1,0:T(8,128)(2,1)S(1)} %get-tuple-element.26), channel_id=1, source_target_pairs={{0,16},{2,18},{4,20},{6,22},{8,24},{10,26},{12,28},{14,30},{16,0},... | collective-permute-start | bytes 1572872 | tf_op jit(solution)/shard_map/ppermute | solution.py:25
  38.4 6.7 %copy-start.28 = (f32[128,64]{0,1:T(8,128)}, f32[128,64]{0,1:T(8,128)S(1)}, u32[]{:S(2)}) copy-start(f32[128,64]{0,1:T(8,128)S(1)} %get-tuple-element.62) | copy-start | bytes 98308
  38.4 91.7 %copy-start.37 = (f32[128,64]{0,1:T(8,128)}, f32[128,64]{0,1:T(8,128)S(1)}, u32[]{:S(2)}) copy-start(f32[128,64]{0,1:T(8,128)S(1)} %get-tuple-element.63) | copy-start | bytes 98308
  38.6 93.6 %copy-start.26 = (f32[128,64]{1,0:T(8,128)}, f32[128,64]{1,0:T(8,128)S(1)}, u32[]{:S(2)}) copy-start(f32[128,64]{1,0:T(8,128)S(1)} %copy.58) | copy-start | bytes 98308
  38.6 27.3 %copy-start.21 = (f32[1,4096]{1,0:T(1,128)S(1)}, f32[1,4096]{1,0:T(1,128)}, u32[]{:S(2)}) copy-start(f32[1,4096]{1,0:T(1,128)} %param.15) | copy-start | bytes 49156
  64.3 159.5 %all-reduce.7.cloned.1.call-start = ((), (), s32[]{:S(2)}) async-start(), calls=%async_computation.9 | async-start | bytes 4194304 | tf_op jit(solution)/shard_map/psum | solution.py:354
  64.4 3.3 copy-start.6
  67.7 8.7 %copy-start.22 = (bf16[1,8,2048]{2,1,0:T(8,128)(2,1)S(1)}, bf16[1,8,2048]{2,1,0:T(8,128)(2,1)}, u32[]{:S(2)}) copy-start(bf16[1,8,2048]{2,1,0:T(8,128)(2,1)} %param.21) | copy-start | bytes 98308
  100.3 5.1 %copy-start.2 = (bf16[128,4096]{1,0:T(8,128)(2,1)S(1)}, bf16[128,4096]{1,0:T(8,128)(2,1)}, u32[]{:S(2)}) copy-start(bf16[128,4096]{1,0:T(8,128)(2,1)} %all-gather.11.cloned.1.call-done) | copy-start | bytes 3145732
  102.5 24.0 %copy-start.64 = (f32[128]{0:T(128)}, f32[128]{0:T(128)S(1)}, u32[]{:S(2)}) copy-start(f32[128]{0:T(128)S(1)} %get-tuple-element.61) | copy-start | bytes 1540
  104.1 9.8 %copy-start.47 = (bf16[128,16]{0,1:T(8,128)(2,1)}, bf16[128,16]{0,1:T(8,128)(2,1)S(1)}, u32[]{:S(2)}) copy-start(bf16[128,16]{0,1:T(8,128)(2,1)S(1)} %convolution_convert_fusion.3) | copy-start | bytes 12292
  126.5 3.7 copy-start.43
  126.5 4.5 copy-start.19
  126.5 4.5 copy-start.36
  126.5 5.8 %copy-start.18 = (f32[128,4,4,64]{3,2,1,0:T(4,128)S(1)}, f32[128,4,4,64]{3,2,1,0:T(4,128)}, u32[]{:S(2)}) copy-start(f32[128,4,4,64]{3,2,1,0:T(4,128)} %get-tuple-element.33) | copy-start | bytes 1572868
  134.6 3.5 copy-start.20
  148.1 23.3 %copy-start.8 = (bf16[128,4,4,128]{0,3,2,1:T(8,128)(2,1)}, bf16[128,4,4,128]{0,3,2,1:T(8,128)(2,1)S(1)}, u32[]{:S(2)}) copy-start(bf16[128,4,4,128]{0,3,2,1:T(8,128)(2,1)S(1)} %copy.79) | copy-start | bytes 1572868
  148.1 24.0 %copy-start.29 = (f32[128,64]{0,1:T(8,128)S(1)}, f32[128,64]{0,1:T(8,128)}, u32[]{:S(2)}) copy-start(f32[128,64]{0,1:T(8,128)} %copy-done.28) | copy-start | bytes 98308
  148.2 24.0 %copy-start.41 = (f32[128,4,128]{0,2,1:T(8,128)S(1)}, f32[128,4,128]{0,2,1:T(8,128)}, u32[]{:S(2)}) copy-start(f32[128,4,128]{0,2,1:T(8,128)} %convolution_bitcast_fusion.7) | copy-start | bytes 786436
  148.2 24.1 %copy-start.39 = (bf16[1,8,512]{2,1,0:T(8,128)(2,1)S(1)}, bf16[1,8,512]{2,1,0:T(8,128)(2,1)}, u32[]{:S(2)}) copy-start(bf16[1,8,512]{2,1,0:T(8,128)(2,1)} %param.22) | copy-start | bytes 24580
  173.0 4.5 %copy-start.3 = (bf16[1,4096,512]{2,1,0:T(8,128)(2,1)S(1)}, bf16[1,4096,512]{2,1,0:T(8,128)(2,1)}, u32[]{:S(2)}) copy-start(bf16[1,4096,512]{2,1,0:T(8,128)(2,1)} %param.18) | copy-start | bytes 12582916
  184.4 9.3 %copy-start.10 = (f32[128,4096]{1,0:T(8,128)S(1)}, f32[128,4096]{1,0:T(8,128)}, u32[]{:S(2)}) copy-start(f32[128,4096]{1,0:T(8,128)} %convolution_add_fusion.4) | copy-start | bytes 6291460
  184.4 9.3 %copy-start.52 = (bf16[128,8]{0,1:T(8,128)(2,1)S(1)}, bf16[128,8]{0,1:T(8,128)(2,1)}, u32[]{:S(2)}) copy-start(bf16[128,8]{0,1:T(8,128)(2,1)} %convolution_convert_fusion.7) | copy-start | bytes 6148
  184.5 9.3 %copy-start.54 = (bf16[128,8]{0,1:T(8,128)(2,1)S(1)}, bf16[128,8]{0,1:T(8,128)(2,1)}, u32[]{:S(2)}) copy-start(bf16[128,8]{0,1:T(8,128)(2,1)} %convolution_convert_fusion.9) | copy-start | bytes 6148
  196.1 46.1 %all-gather.15.cloned.1.call-start = ((), (), s32[]{:S(2)}) async-start(), calls=%async_computation.4 | async-start | bytes 1572864 | tf_op jit(solution)/shard_map/all_gather | solution.py:341
  196.7 102.2 %all-gather.19.cloned.1.call-start = ((), (), s32[]{:S(2)}) async-start(), calls=%async_computation.6 | async-start | bytes 1572864 | tf_op jit(solution)/shard_map/all_gather | solution.py:343
  197.4 201.7 %reduce-scatter.2.cloned.1.call-start = ((), (), s32[]{:S(2)}) async-start(), calls=%async_computation.3 | async-start | bytes 196608 | tf_op jit(solution)/shard_map/reduce_scatter | solution.py:428
  197.5 6.4 %copy-start.1 = (bf16[128,4096]{1,0:T(8,128)(2,1)S(1)}, bf16[128,4096]{1,0:T(8,128)(2,1)}, u32[]{:S(2)}) copy-start(bf16[128,4096]{1,0:T(8,128)(2,1)} %all-gather.13.cloned.1.call-done) | copy-start | bytes 3145732
  199.7 4.2 copy-start.60
  218.0 4.4 copy-start.4
  218.0 4.4 copy-start.44
  223.8 6.5 %copy-start.53 = (bf16[128,8]{0,1:T(8,128)(2,1)S(1)}, bf16[128,8]{0,1:T(8,128)(2,1)}, u32[]{:S(2)}) copy-start(bf16[128,8]{0,1:T(8,128)(2,1)} %convolution_convert_fusion.7) | copy-start | bytes 6148
  223.8 6.5 %copy-start.55 = (bf16[128,8]{0,1:T(8,128)(2,1)S(1)}, bf16[128,8]{0,1:T(8,128)(2,1)}, u32[]{:S(2)}) copy-start(bf16[128,8]{0,1:T(8,128)(2,1)} %convolution_convert_fusion.9) | copy-start | bytes 6148
  223.8 6.5 %copy-start.66 = (f32[128]{0:T(128)S(1)}, f32[128]{0:T(128)}, u32[]{:S(2)}) copy-start(f32[128]{0:T(128)} %copy-done.64) | copy-start | bytes 1540
  226.3 46.5 %collective-permute-start = (bf16[128,4096]{1,0:T(8,128)(2,1)}, bf16[128,4096]{1,0:T(8,128)(2,1)}, u32[]{:S(2)}, u32[]{:S(2)}) collective-permute-start(bf16[128,4096]{1,0:T(8,128)(2,1)} %fusion.64), channel_id=1, source_target_pairs={{0,2},{2,4},{4,6},{6,8},{8,10},{10,12},{12,14},{14,16},{16,18},{18... | collective-permute-start | bytes 3145736 | tf_op jit(solution)/shard_map/ppermute | solution.py:19
  231.5 6.5 %copy-start.13 = (bf16[1,128,4096]{2,1,0:T(8,128)(2,1)S(1)}, bf16[1,128,4096]{2,1,0:T(8,128)(2,1)}, u32[]{:S(2)}) copy-start(bf16[1,128,4096]{2,1,0:T(8,128)(2,1)} %all-gather.21.cloned.1.call-done) | copy-start | bytes 3145732
  240.5 58.4 %collective-permute-start.2 = (bf16[128,4096]{1,0:T(8,128)(2,1)}, bf16[128,4096]{1,0:T(8,128)(2,1)}, u32[]{:S(2)}, u32[]{:S(2)}) collective-permute-start(bf16[128,4096]{1,0:T(8,128)(2,1)} %add_convert_fusion), channel_id=1, source_target_pairs={{2,0},{4,2},{6,4},{8,6},{10,8},{12,10},{14,12},{16,14},{18,16},{20... | collective-permute-start | bytes 3145736 | tf_op jit(solution)/shard_map/ppermute | solution.py:19
  274.6 8.2 %copy-start.69 = (f32[128]{0:T(128)}, f32[128]{0:T(128)S(1)}, u32[]{:S(2)}) copy-start(f32[128]{0:T(128)S(1)} %add_rsqrt_fusion.2) | copy-start | bytes 1540
  316.1 4.5 copy-start.14
  316.1 4.5 copy-start.15
  316.1 4.5 copy-start.27
  344.3 15.1 %copy-start.56 = (bf16[128,8]{0,1:T(8,128)(2,1)}, bf16[128,8]{0,1:T(8,128)(2,1)S(1)}, u32[]{:S(2)}) copy-start(bf16[128,8]{0,1:T(8,128)(2,1)S(1)} %convolution_convert_fusion.6) | copy-start | bytes 6148
  344.3 13.1 %copy-start.40 = (bf16[1,8,512]{2,1,0:T(8,128)(2,1)S(1)}, bf16[1,8,512]{2,1,0:T(8,128)(2,1)}, u32[]{:S(2)}) copy-start(bf16[1,8,512]{2,1,0:T(8,128)(2,1)} %param.22) | copy-start | bytes 24580
  344.3 13.1 %copy-start.68 = (bf16[128,16]{0,1:T(8,128)(2,1)S(1)}, bf16[128,16]{0,1:T(8,128)(2,1)}, u32[]{:S(2)}) copy-start(bf16[128,16]{0,1:T(8,128)(2,1)} %copy-done.67) | copy-start | bytes 12292
  344.3 15.0 %copy-start.62 = (f32[128]{0:T(128)S(1)}, f32[128]{0:T(128)}, u32[]{:S(2)}) copy-start(f32[128]{0:T(128)} %copy-done.60) | copy-start | bytes 1540
  357.4 4.1 copy-start.30
  361.4 78.5 %all-reduce.5.cloned.1.call-start = ((), (), s32[]{:S(2)}) async-start(), calls=%async_computation.8 | async-start | bytes 4194304 | tf_op jit(solution)/shard_map/psum | solution.py:354
  362.5 4.5 %copy-start.5 = (bf16[1,4096,512]{2,1,0:T(8,128)(2,1)S(1)}, bf16[1,4096,512]{2,1,0:T(8,128)(2,1)}, u32[]{:S(2)}) copy-start(bf16[1,4096,512]{2,1,0:T(8,128)(2,1)} %param.18) | copy-start | bytes 12582916
  362.5 4.5 %copy-start.23 = (bf16[4,128,128]{1,2,0:T(8,128)(2,1)S(1)}, bf16[4,128,128]{1,2,0:T(8,128)(2,1)}, u32[]{:S(2)}) copy-start(bf16[4,128,128]{1,2,0:T(8,128)(2,1)} %fusion.114) | copy-start | bytes 393220
  370.6 3.1 copy-start.45
  378.5 3.2 copy-start.25
  391.7 37.2 %collective-permute-start.4 = (bf16[128,2048]{1,0:T(8,128)(2,1)}, bf16[128,2048]{1,0:T(8,128)(2,1)}, u32[]{:S(2)}, u32[]{:S(2)}) collective-permute-start(bf16[128,2048]{1,0:T(8,128)(2,1)} %dynamic-slice_bitcast_fusion), channel_id=1, source_target_pairs={{0,16},{2,18},{4,20},{6,22},{8,24},{10,26},{12,28},{14,30},{16,0},... | collective-permute-start | bytes 1572872 | tf_op jit(solution)/shard_map/ppermute | solution.py:25
  392.4 5.0 %copy-start.7 = (bf16[128,4,4,128]{0,3,2,1:T(8,128)(2,1)S(1)}, bf16[128,4,4,128]{0,3,2,1:T(8,128)(2,1)}, u32[]{:S(2)}) copy-start(bf16[128,4,4,128]{0,3,2,1:T(8,128)(2,1)} %copy.93) | copy-start | bytes 1572868
  392.4 5.0 %copy-start.50 = (bf16[128,16]{0,1:T(8,128)(2,1)S(1)}, bf16[128,16]{0,1:T(8,128)(2,1)}, u32[]{:S(2)}) copy-start(bf16[128,16]{0,1:T(8,128)(2,1)} %copy-done.49) | copy-start | bytes 12292
  392.4 5.9 %copy-start.24 = (bf16[4,128,128]{1,2,0:T(8,128)(2,1)S(1)}, bf16[4,128,128]{1,2,0:T(8,128)(2,1)}, u32[]{:S(2)}) copy-start(bf16[4,128,128]{1,2,0:T(8,128)(2,1)} %fusion.114) | copy-start | bytes 393220
  394.0 45.9 %copy-start.11 = (bf16[128,4096]{1,0:T(8,128)(2,1)S(1)}, bf16[128,4096]{1,0:T(8,128)(2,1)}, u32[]{:S(2)}) copy-start(bf16[128,4096]{1,0:T(8,128)(2,1)} %bitcast_select_fusion) | copy-start | bytes 3145732
  394.9 42.8 %collective-permute-start.5 = (bf16[128,2048]{1,0:T(8,128)(2,1)}, bf16[128,2048]{1,0:T(8,128)(2,1)}, u32[]{:S(2)}, u32[]{:S(2)}) collective-permute-start(bf16[128,2048]{1,0:T(8,128)(2,1)} %constant_dynamic-slice_fusion), channel_id=1, source_target_pairs={{0,16},{2,18},{4,20},{6,22},{8,24},{10,26},{12,28},{14,30},{16,0},... | collective-permute-start | bytes 1572872 | tf_op jit(solution)/shard_map/ppermute | solution.py:25
  398.3 43.5 %copy-start.12 = (f32[128,4096]{1,0:T(8,128)S(1)}, f32[128,4096]{1,0:T(8,128)}, u32[]{:S(2)}) copy-start(f32[128,4096]{1,0:T(8,128)} %convert_element_type.245) | copy-start | bytes 6291460
  (24 other events, 43.7 us)
Sparse Core Ops, SparseCore 0:
  9.6 11.7 all-gather.16
  22.9 10.1 all-gather.20
  38.2 10.2 all-gather.10
  64.4 7.6 all-gather.12
  196.2 19.7 all-reduce.6
  217.5 10.2 all-gather.14
  229.3 10.1 all-gather.18
  361.5 6.2 reduce-scatter.1
  391.0 20.0 all-reduce.4
where the time goes:
time: 457 us; the launch traced here: 451 us
  matrix products  214 us (47%)
  waiting for transfers between devices  108 us (24%)
  local copies, waits for them, and re-layouts  54.8 us (12%)
  other arithmetic  45 us (10%)
  between operations  14.9 us (3%)
  starting transfers between devices  13.2 us (3%)
    ppermute x4, waiting for transfers between devices, partner(): return lax.ppermute(value, axis, pairs)  74.9 us
    dot_general x2, matrix products, section_backward_pass(): lax.dot_general(query_grad, query_weight_matrix, last_dims, preferred_ele...  36.3 us
    dot_general x4, matrix products, apply_projection(): jnp.dot(normalized_input, query_weight_matrix, preferred_element_type=jnp...  34.5 us
    ppermute x2, waiting for transfers between devices, passed_along(): return lax.ppermute(block, axis, route)  30.7 us
    dot_general x2, matrix products, section_backward_pass(): lax.dot_general(incoming_cotangent, output_weight_matrix, last_dims, pref...  24.3 us
    dot_general x2, matrix products, section_loss_term(): jnp.dot(context, output_weight_matrix, preferred_element_type=jnp.float32)  18.4 us
    dot_general x4, matrix products, apply_projection(): jnp.dot(normalized_input, key_weight_matrix, preferred_element_type=jnp.f...  16.5 us
    unnamed x152, local copies, waits for them, and re-layouts  16.1 us
  transfers between devices with their start and end apart: 15, of which 5 were waited for; matrix products, arithmetic and copies ran while one was open for 54% of the time, Pallas kernels for 0%

commit v1 on v0

v1 whole, which is shorter than its diff:
```python
import functools
import math

import jax
import jax.numpy as jnp
import numpy as np
from jax import lax
from jax.experimental import pallas as pl
from jax.experimental.pallas import tpu as pltpu
from jax.sharding import PartitionSpec as P

HEAD = 128
eps = 1e-05
rope_base = 500000.0
mask_fill = -1e30
BLOCK = 16
f32 = jnp.float32
bf16 = jnp.bfloat16


def rope_tables(row_count):
    half = HEAD // 2
    exponent = np.arange(half, dtype=np.float32) * np.float32(2.0 / HEAD)
    frequency = np.exp(-exponent * np.float32(math.log(rope_base)))
    angles = np.arange(row_count, dtype=np.float32)[:, None] * frequency[None, :]
    cosines, sines = np.cos(angles), np.sin(angles)
    return (
        np.concatenate([cosines, cosines], 1).astype(np.float32),
        np.concatenate([-sines, sines], 1).astype(np.float32),
    )


def dot(a, b):
    return jnp.dot(a, b, preferred_element_type=f32)


def dot_nt(a, b):
    return lax.dot_general(a, b, (((1,), (1,)), ((), ())), preferred_element_type=f32)


def dot_tn(a, b):
    return lax.dot_general(a, b, (((0,), (0,)), ((), ())), preferred_element_type=f32)


def cols(start, size):
    return pl.ds(pl.multiple_of(start, 128), size)


def loop(count, body):
    def step(i, carry):
        body(i)
        return carry

    lax.fori_loop(0, count, step, 0)


def kernel(
    sections,
    shares,
    gain,
    down,
    qup,
    vup,
    cos_ref,
    sin_ref,
    fids,
    bids,
    wq_hbm,
    wk_hbm,
    wv_hbm,
    wo_hbm,
    arriving,
    entering,
    returning,
    head_grad,
    parked,
    departing,
    returned,
    parked_out,
    g_down,
    g_query,
    g_value,
    wq,
    wk,
    wv,
    wo,
    x0,
    x1,
    p0,
    p1,
    c0,
    c1,
    nrm,
    rms,
    q,
    k,
    v,
    ctx,
    dctx,
    dk,
    dv,
    dn,
    part,
    recv,
    res,
    gd,
    gd_send,
    gd_recv,
    mask,
    w_sem,
    l_sem,
    gs_sem,
    gr_sem,
    cs_sem,
    cr_sem,
    hs_sem,
    hr_sem,
):
    rows, width = x0.shape
    share = width // shares
    dq_width = wq.shape[1]
    kv_width = wk.shape[1]
    groups = kv_width // HEAD
    per = dq_width // kv_width
    inverse = 1.0 / math.sqrt(HEAD)
    s = lax.axis_index("section")
    me = lax.axis_index("tensor")
    half = sections // 2
    mate = jnp.where(s < half, s + half, s - half)
    own = cols(me * share, share)
    q_step = min(512, dq_width)
    f_step = min(512, width)
    MESH = pl.DeviceIdType.MESH

    def peer(d):
        return lax.rem(me + d, shares)

    barrier = pltpu.get_barrier_semaphore()
    for d in range(1, shares):
        pl.semaphore_signal(barrier, inc=1, device_id=(s, peer(d)), device_id_type=MESH)
    pl.semaphore_signal(barrier, inc=1, device_id=(mate, me), device_id_type=MESH)

    for other in (lax.rem(s + 1, sections), lax.rem(s + sections - 1, sections)):
        pl.semaphore_signal(barrier, inc=1, device_id=(other, me), device_id_type=MESH)

    x0_local = pltpu.make_async_copy(arriving.at[0], x0.at[:, own], l_sem.at[0])
    c0_local = pltpu.make_async_copy(returning.at[0], c0.at[:, own], l_sem.at[1])
    x1_local = pltpu.make_async_copy(entering.at[0], x1.at[:, own], l_sem.at[2])
    c1_local = pltpu.make_async_copy(head_grad.at[0], c1.at[:, own], l_sem.at[3])
    x0_local.start()
    wk_copy = pltpu.make_async_copy(wk_hbm.at[0], wk, w_sem.at[0])
    wv_copy = pltpu.make_async_copy(wv_hbm.at[0], wv, w_sem.at[1])
    wk_copy.start()
    wv_copy.start()

    def wq_copy(i):
        piece = cols(i * q_step, q_step)
        return pltpu.make_async_copy(wq_hbm.at[0, :, piece], wq.at[:, piece], w_sem.at[2 + i])

    q_pieces = dq_width // q_step
    f_pieces = width // f_step

    def wo_copy(i):
        piece = cols(i * f_step, f_step)
        return pltpu.make_async_copy(
            wo_hbm.at[0, :, piece], wo.at[:, piece], w_sem.at[2 + q_pieces + i]
        )

    pl.semaphore_wait(barrier, shares + 2)

    def remote(source, target, send, receive, section, tensor):
        return pltpu.make_async_remote_copy(
            src_ref=source,
            dst_ref=target,
            send_sem=send,
            recv_sem=receive,
            device_id=(section, tensor),
            device_id_type=MESH,
        )

    def gather(source, buffer, slot):
        return [
            remote(
                source,
                buffer.at[:, own],
                gs_sem.at[slot, d - 1],
                gr_sem.at[slot, d - 1],
                s,
                peer(d),
            )
            for d in range(1, shares)
        ]

    def hop(source, target, slot, section):
        return remote(source, target, hs_sem.at[slot], hr_sem.at[slot], section, me)

    def start(copies):
        for copy in copies:
            copy.start()

    def wait(copies):
        for copy in copies:
            copy.wait()

    x0_gather = gather(arriving.at[0], x0, 0)
    c0_gather = gather(returning.at[0], c0, 1)
    x1_gather = gather(x1.at[:, own], x1, 2)
    c1_gather = gather(c1.at[:, own], c1, 3)
    p0_gather = gather(p0.at[:, own], p0, 4)
    p1_gather = gather(p1.at[:, own], p1, 5)
    p0_hop = hop(parked.at[0, 0], p0.at[:, own], 0, mate)
    p1_hop = hop(parked.at[0, 1], p1.at[:, own], 1, mate)
    s0_hop = hop(arriving.at[0], parked_out.at[0, 0], 2, mate)
    s1_hop = hop(x1.at[:, own], parked_out.at[0, 1], 3, mate)
    forth_hop = hop(res.at[0], x1.at[:, own], 4, lax.rem(s + 1, sections))
    back_hop = hop(res.at[1], c1.at[:, own], 5, lax.rem(s + sections - 1, sections))

    start(x0_gather)
    p0_hop.start()
    for i in range(q_pieces):
        wq_copy(i).start()
    for i in range(f_pieces):
        wo_copy(i).start()
    start(c0_gather)
    c0_local.start()

    @pl.when(s == 0)
    def _():
        x1_local.start()

    @pl.when(s == sections - 1)
    def _():
        c1_local.start()

    def rotate(value, direction):
        return value * cos_ref[...] + pltpu.roll(value, HEAD // 2, 1) * (
            sin_ref[...] * direction
        )

    def make_mask(ids, index):
        along = jnp.broadcast_to(ids[pl.ds(index, 1), :].astype(f32), (rows, rows))
        down_rows = along.T
        row = lax.broadcasted_iota(jnp.int32, (rows, rows), 0)
        column = lax.broadcasted_iota(jnp.int32, (rows, rows), 1)
        keep = (column <= row) & (along == down_rows)
        mask[...] = jnp.where(keep, 1, 0).astype(jnp.int32)

    def project(x, first):
        def norm(b):
            at = pl.ds(pl.multiple_of(b * BLOCK, BLOCK), BLOCK)
            value = x[at, :].astype(f32)
            r = lax.rsqrt(jnp.mean(value * value, axis=1, keepdims=True) + eps)
            rms[at, :] = jnp.broadcast_to(r, (BLOCK, HEAD))
            nrm[at, :] = (value * r * gain[...]).astype(bf16)

        loop(rows // BLOCK, norm)
        low = dot_nt(nrm[...], down[...]).astype(bf16)
        if first:
            wk_copy.wait()

        kv_step = min(256, kv_width)

        def keys(i):
            out = dot(nrm[...], wk[:, cols(i * kv_step, kv_step)])
            for j in range(kv_step // HEAD):
                k[:, cols(i * kv_step + j * HEAD, HEAD)] = rotate(
                    out[:, j * HEAD : (j + 1) * HEAD], 1.0
                ).astype(bf16)

        loop(kv_width // kv_step, keys)
        if first:
            wv_copy.wait()

        def values(i):
            at = cols(i * kv_step, kv_step)
            v[:, at] = (dot(nrm[...], wv[:, at]) + dot(low, vup[:, at])).astype(bf16)

        loop(kv_width // kv_step, values)

        def queries(i):
            if first:
                wq_copy(i).wait()
            at = cols(i * q_step, q_step)
            out = dot(nrm[...], wq[:, at]) + dot(low, qup[:, at])
            for j in range(q_step // HEAD):
                q[:, cols(i * q_step + j * HEAD, HEAD)] = rotate(
                    out[:, j * HEAD : (j + 1) * HEAD], 1.0
                ).astype(bf16)

        loop(q_pieces, queries)

    def stack(ref, g):
        return jnp.concatenate(
            [ref[:, cols((g * per + j) * HEAD, HEAD)] for j in range(per)], axis=0
        )

    def softmax(q4, kk):
        scores = dot_nt(q4, kk) * inverse
        allowed = jnp.concatenate([mask[...]] * per, axis=0)
        scores = jnp.where(allowed > 0, scores, mask_fill)
        weights = jnp.exp(scores - jnp.max(scores, axis=1, keepdims=True))
        return weights / jnp.sum(weights, axis=1, keepdims=True)

    def exchange(base, target, slot):
        copies = [
            remote(
                part.at[:, cols(peer(d) * share, share)],
                recv.at[slot, d - 1],
                cs_sem.at[slot, d - 1],
                cr_sem.at[slot, d - 1],
                s,
                peer(d),
            )
            for d in range(1, shares)
        ]
        start(copies)
        wait(copies)

        def add(b):
            at = pl.ds(pl.multiple_of(b * BLOCK, BLOCK), BLOCK)
            total = part[at, own].astype(f32)
            for d in range(1, shares):
                total = total + recv[slot, d - 1, at, :].astype(f32)
            target[at, :] = (base[at, own].astype(f32) + total).astype(bf16)

        loop(rows // BLOCK, add)

    def forward(x, ids, index, target, slot, first):
        make_mask(ids, index)
        project(x, first)

        def attend(g):
            probs = softmax(stack(q, g), k[:, cols(g * HEAD, HEAD)])
            out = dot(probs.astype(bf16), v[:, cols(g * HEAD, HEAD)]).astype(bf16)
            for j in range(per):
                ctx[:, cols((g * per + j) * HEAD, HEAD)] = out[j * rows : (j + 1) * rows]

        loop(groups, attend)

        def output(i):
            if first:
                wo_copy(i).wait()
            at = cols(i * f_step, f_step)
            part[:, at] = dot(ctx[...], wo[:, at]).astype(bf16)

        loop(f_pieces, output)
        exchange(x, target, slot)

    def backward(x, c, ids, index, target, slot, first):
        make_mask(ids, index)
        project(x, False)
        low_t = dot_nt(down[...], nrm[...]).astype(bf16)

        c_step = min(512, dq_width)

        def contexts(i):
            at = cols(i * c_step, c_step)
            dctx[:, at] = dot_nt(c[...], wo[at, :]).astype(bf16)

        loop(dq_width // c_step, contexts)

        def attend(g):
            at = cols(g * HEAD, HEAD)
            q4, kk, dc4 = stack(q, g), k[:, at], stack(dctx, g)
            probs = softmax(q4, kk)
            d_probs = dot_nt(dc4, v[:, at])
            dv[:, at] = dot_tn(probs.astype(bf16), dc4).astype(bf16)
            d_score = (
                probs * (d_probs - jnp.sum(d_probs * probs, axis=1, keepdims=True)) * inverse
            ).astype(bf16)
            dq4 = dot(d_score, kk)
            dk[:, at] = rotate(dot_tn(d_score, q4), -1.0).astype(bf16)
            for j in range(per):
                ctx[:, cols((g * per + j) * HEAD, HEAD)] = rotate(
                    dq4[j * rows : (j + 1) * rows], -1.0
                ).astype(bf16)

        loop(groups, attend)
        d_low = (dot_nt(ctx[...], qup[...]) + dot_nt(dv[...], vup[...])).astype(bf16)
        d_low_t = (dot_nt(qup[...], ctx[...]) + dot_nt(vup[...], dv[...])).astype(bf16)

        def normed(i):
            at = cols(i * f_step, f_step)
            dn[:, at] = (
                dot_nt(ctx[...], wq[at, :])
                + dot_nt(dk[...], wk[at, :])
                + dot_nt(dv[...], wv[at, :])
                + dot(d_low, down[:, at])
            )

        loop(f_pieces, normed)

        def inputs(b):
            at = pl.ds(pl.multiple_of(b * BLOCK, BLOCK), BLOCK)
            r = rms[at, 0:1]
            weighted = dn[at, :] * gain[...]
            value = x[at, :].astype(f32)
            mean = jnp.mean(value * weighted, axis=1, keepdims=True)
            part[at, :] = (r * weighted - value * (r * r * r * mean)).astype(bf16)

        loop(rows // BLOCK, inputs)
        exchange(c, target, slot)

        rank = g_query.shape[1]
        up_q = dot(low_t, ctx[...])[:rank]
        up_v = dot(low_t, dv[...])[rank:]
        g_query[0] = up_q if first else g_query[0] + up_q
        g_value[0] = up_v if first else g_value[0] + up_v

        def downs(i):
            at = cols(i * f_step, f_step)
            value = dot(d_low_t, nrm[:, at])
            gd[:, at] = value if first else gd[:, at] + value

        return functools.partial(loop, f_pieces, downs)

    x0_local.wait()
    wait(x0_gather)
    forward(x0, fids, sections - 1 - s, res.at[0], 0, True)

    @pl.when(s < sections - 1)
    def _():
        forth_hop.start()

    p0_hop.wait()
    p1_hop.start()
    s0_hop.start()
    start(p0_gather)
    c0_local.wait()
    wait(c0_gather)
    wait(p0_gather)

    backward(p0, c0, bids, s, res.at[1], 2, True)()

    @pl.when(s > 0)
    def _():
        back_hop.start()
        forth_hop.wait_recv()

    @pl.when(s == 0)
    def _():
        x1_local.wait()

    start(x1_gather)
    s1_hop.start()
    wait(x1_gather)

    forward(x1, fids, sections - s, departing.at[0], 1, False)

    p1_hop.wait()
    start(p1_gather)

    @pl.when(s < sections - 1)
    def _():
        back_hop.wait_recv()

    @pl.when(s == sections - 1)
    def _():
        c1_local.wait()

    start(c1_gather)
    wait(p1_gather)
    wait(c1_gather)

    backward(p1, c1, bids, s + 1, returned.at[0], 3, False)()

    gd_send[...] = gd[...].astype(bf16)
    copies = [
        remote(
            gd_send.at[:, cols(peer(d) * share, share)],
            gd_recv.at[d - 1],
            gs_sem.at[6, d - 1],
            gr_sem.at[6, d - 1],
            s,
            peer(d),
        )
        for d in range(1, shares)
    ]
    start(copies)
    wait(copies)
    total = gd[:, own]
    for d in range(1, shares):
        total = total + gd_recv[d - 1].astype(f32)
    rank = g_query.shape[1]
    g_down[0, 0] = total[:rank]
    g_down[0, 1] = total[rank:]

    @pl.when(s < sections - 1)
    def _():
        forth_hop.wait_send()

    @pl.when(s > 0)
    def _():
        back_hop.wait_send()

    s0_hop.wait()
    s1_hop.wait()


def per_device(
    gain, wq, wk, wv, wo, down, qup, vup, arriving, entering, returning, head_grad, parked,
    fids, bids,
):
    sections = lax.axis_size("section")
    shares = lax.axis_size("tensor")
    rows, share = arriving.shape[1:]
    width = share * shares
    dq_width, kv_width = wq.shape[2], wk.shape[2]
    rank = qup.shape[1]
    cosines, sines = rope_tables(rows)
    zeros_q, zeros_v = jnp.zeros_like(qup[0]), jnp.zeros_like(vup[0])
    qup_wide = jnp.concatenate([qup[0], zeros_q], axis=0)
    vup_wide = jnp.concatenate([zeros_v, vup[0]], axis=0)
    down_flat = down.reshape(2 * rank, width)
    vmem = pl.BlockSpec(memory_space=pltpu.VMEM)
    anywhere = pl.BlockSpec(memory_space=pl.ANY)
    others = max(shares - 1, 1)
    pieces = 2 + dq_width // min(512, dq_width) + width // min(512, width)
    act = pltpu.VMEM((rows, width), bf16)
    return pl.pallas_call(
        functools.partial(kernel, sections, shares),
        out_shape=(
            jax.ShapeDtypeStruct((1, rows, share), bf16),
            jax.ShapeDtypeStruct((1, rows, share), bf16),
            jax.ShapeDtypeStruct(parked.shape, bf16),
            jax.ShapeDtypeStruct((1, 2, rank, share), f32),
            jax.ShapeDtypeStruct((1, rank, dq_width), f32),
            jax.ShapeDtypeStruct((1, rank, kv_width), f32),
        ),
        in_specs=[vmem] * 8 + [anywhere] * 9,
        out_specs=(vmem, vmem, anywhere, vmem, vmem, vmem),
        scratch_shapes=[
            pltpu.VMEM(wq.shape[1:], bf16),
            pltpu.VMEM(wk.shape[1:], bf16),
            pltpu.VMEM(wv.shape[1:], bf16),
            pltpu.VMEM(wo.shape[1:], bf16),
            act, act, act, act, act, act,
            act,
            pltpu.VMEM((rows, HEAD), f32),
            pltpu.VMEM((rows, dq_width), bf16),
            pltpu.VMEM((rows, kv_width), bf16),
            pltpu.VMEM((rows, kv_width), bf16),
            pltpu.VMEM((rows, dq_width), bf16),
            pltpu.VMEM((rows, dq_width), bf16),
            pltpu.VMEM((rows, kv_width), bf16),
            pltpu.VMEM((rows, kv_width), bf16),
            pltpu.VMEM((rows, width), f32),
            act,
            pltpu.VMEM((4, others, rows, share), bf16),
            pltpu.VMEM((2, rows, share), bf16),
            pltpu.VMEM((2 * rank, width), f32),
            pltpu.VMEM((2 * rank, width), bf16),
            pltpu.VMEM((others, 2 * rank, share), bf16),
            pltpu.VMEM((rows, rows), jnp.int32),
            pltpu.SemaphoreType.DMA((pieces,)),
            pltpu.SemaphoreType.DMA((4,)),
            pltpu.SemaphoreType.DMA((7, others)),
            pltpu.SemaphoreType.DMA((7, others)),
            pltpu.SemaphoreType.DMA((4, others)),
            pltpu.SemaphoreType.DMA((4, others)),
            pltpu.SemaphoreType.DMA((6,)),
            pltpu.SemaphoreType.DMA((6,)),
        ],
        compiler_params=pltpu.CompilerParams(
            collective_id=0, has_side_effects=True, vmem_limit_bytes=63 * 2**20
        ),
    )(
        gain, down_flat, qup_wide, vup_wide, jnp.asarray(cosines), jnp.asarray(sines),
        fids, bids, wq, wk, wv, wo, arriving, entering, returning, head_grad, parked,
    )


def solution(mesh):
    by_share = P("section", None, "tensor")
    placed = (
        P("section", None), by_share, by_share, by_share,
        P("section", "tensor", None), P("section", None, None, None), by_share, by_share,
        by_share, P(None, None, "tensor"), by_share, P(None, None, "tensor"),
        P("section", None, None, "tensor"), P(), P(),
    )
    return jax.shard_map(
        per_device,
        mesh=mesh,
        in_specs=placed,
        out_specs=(
            by_share, by_share, P("section", None, None, "tensor"),
            P("section", None, None, "tensor"), by_share, by_share,
        ),
        check_vma=False,
    )
```

time: 457 us -> 148 us (0.32)
  the two profiles are of different devices: /device:TPU:0 before, /device:TPU:15 now
where the time goes in v1:
time: 148 us; the launch traced here: 147 us
  Pallas kernels  134 us (91%)
  local copies, waits for them, and re-layouts  13.1 us (9%)
    pallas_call x1, Pallas kernels, per_device(): pl.pallas_call(functools.partial(kernel, sections, shares), out_shape=(ja...  134 us
    unnamed x6, local copies, waits for them, and re-layouts  10.4 us

profile of v1, /device:TPU:15, one launch (start us, length us, event | category | flops | bytes accessed | tf_op | source)
XLA Modules:
  0.0 147.4 jit_solution(12392898073126102323)
XLA Ops:
  0.6 1.3 concatenate.7.vup
  1.9 1.4 concatenate.6.qup
  3.3 133.6 %shard_map.208 = (bf16[1,128,2048]{2,1,0:T(8,128)(2,1)}, bf16[1,128,2048]{2,1,0:T(8,128)(2,1)}, bf16[1,2,128,2048]{3,2,1,0:T(8,128)(2,1)}, f32[1,2,8,2048]{3,2,1...) custom-call(f32[1,4096]{1,0:T(1,128)} %gain.1, bf16[16,4096]{1,0:T(8,128)(2,1)} %bitcast.3, ...), custom_call_target="tpu_custom_call" | custom-call | tf_op jit(solution)/shard_map/pallas_call | solution.py:520
  137.0 1.9 %copy.29 = bf16[1,128,2048]{2,1,0:T(8,128)(2,1)} copy(bf16[1,128,2048]{2,1,0:T(8,128)(2,1)} %get-tuple-element.12) | data formatting | bytes 1048576
  138.8 1.9 %copy.30 = bf16[1,128,2048]{2,1,0:T(8,128)(2,1)} copy(bf16[1,128,2048]{2,1,0:T(8,128)(2,1)} %get-tuple-element.13) | data formatting | bytes 1048576
  140.7 2.3 %copy.31 = bf16[1,2,128,2048]{3,2,1,0:T(8,128)(2,1)} copy(bf16[1,2,128,2048]{3,2,1,0:T(8,128)(2,1)} %get-tuple-element.14) | data formatting | bytes 2097152
  143.0 1.6 %copy.32 = f32[1,2,8,2048]{3,2,1,0:T(8,128)} copy(f32[1,2,8,2048]{3,2,1,0:T(8,128)} %get-tuple-element.15) | data formatting | bytes 262144
  144.6 1.5 copy.33
  146.1 1.3 copy.34

commit v2 on v1

--- a/solution.py
+++ b/solution.py
@@ -59,8 +59,8 @@
     shares,
     gain,
     down,
-    qup,
-    vup,
+    qup_in,
+    vup_in,
     cos_ref,
     sin_ref,
     fids,
@@ -107,6 +107,8 @@
     gd_send,
     gd_recv,
     mask,
+    qup,
+    vup,
     w_sem,
     l_sem,
     gs_sem,
@@ -129,7 +131,7 @@
     mate = jnp.where(s < half, s + half, s - half)
     own = cols(me * share, share)
     q_step = min(512, dq_width)
-    f_step = min(512, width)
+    f_step = min(512, share)
     MESH = pl.DeviceIdType.MESH
 
     def peer(d):
@@ -223,6 +225,9 @@
         wo_copy(i).start()
     start(c0_gather)
     c0_local.start()
+    up_q_rows, up_v_rows = qup_in[0].astype(f32), vup_in[0].astype(f32)
+    qup[...] = jnp.concatenate([up_q_rows, jnp.zeros_like(up_q_rows)], axis=0).astype(bf16)
+    vup[...] = jnp.concatenate([jnp.zeros_like(up_v_rows), up_v_rows], axis=0).astype(bf16)
 
     @pl.when(s == 0)
     def _():
@@ -301,8 +306,8 @@
         weights = jnp.exp(scores - jnp.max(scores, axis=1, keepdims=True))
         return weights / jnp.sum(weights, axis=1, keepdims=True)
 
-    def exchange(base, target, slot):
-        copies = [
+    def sends(slot):
+        return [
             remote(
                 part.at[:, cols(peer(d) * share, share)],
                 recv.at[slot, d - 1],
@@ -313,7 +318,8 @@
             )
             for d in range(1, shares)
         ]
-        start(copies)
+
+    def merge(base, target, slot, copies):
         wait(copies)
 
         def add(b):
@@ -325,7 +331,7 @@
 
         loop(rows // BLOCK, add)
 
-    def forward(x, ids, index, target, slot, first):
+    def forward(x, ids, index, target, slot, first, between):
         make_mask(ids, index)
         project(x, first)
 
@@ -336,28 +342,39 @@
                 ctx[:, cols((g * per + j) * HEAD, HEAD)] = out[j * rows : (j + 1) * rows]
 
         loop(groups, attend)
-
-        def output(i):
-            if first:
-                wo_copy(i).wait()
-            at = cols(i * f_step, f_step)
-            part[:, at] = dot(ctx[...], wo[:, at]).astype(bf16)
-
-        loop(f_pieces, output)
-        exchange(x, target, slot)
-
-    def backward(x, c, ids, index, target, slot, first):
+        between()
+
+        copies = sends(slot)
+        for d in range(1, shares + 1):
+
+            def output(i):
+                piece = peer(d) * (share // f_step) + i
+                if first:
+                    wo_copy(piece).wait()
+                at = cols(piece * f_step, f_step)
+                part[:, at] = dot(ctx[...], wo[:, at]).astype(bf16)
+
+            loop(share // f_step, output)
+            if d < shares:
+                copies[d - 1].start()
+        merge(x, target, slot, copies)
+
+    def backward(x, c, ids, index, target, slot, first, arrive, between):
         make_mask(ids, index)
-        project(x, False)
-        low_t = dot_nt(down[...], nrm[...]).astype(bf16)
-
         c_step = min(512, dq_width)
 
         def contexts(i):
             at = cols(i * c_step, c_step)
             dctx[:, at] = dot_nt(c[...], wo[at, :]).astype(bf16)
 
-        loop(dq_width // c_step, contexts)
+        pieces = dq_width // c_step
+        early = pieces // 2
+        loop(early, contexts)
+        arrive()
+        loop(pieces - early, lambda i: contexts(early + i))
+        wait(p0_gather if first else p1_gather)
+        project(x, False)
+        low_t = dot_nt(down[...], nrm[...]).astype(bf16)
 
         def attend(g):
             at = cols(g * HEAD, HEAD)
@@ -376,6 +393,7 @@
                 ).astype(bf16)
 
         loop(groups, attend)
+        between()
         d_low = (dot_nt(ctx[...], qup[...]) + dot_nt(dv[...], vup[...])).astype(bf16)
         d_low_t = (dot_nt(qup[...], ctx[...]) + dot_nt(vup[...], dv[...])).astype(bf16)
 
@@ -399,7 +417,8 @@
             part[at, :] = (r * weighted - value * (r * r * r * mean)).astype(bf16)
 
         loop(rows // BLOCK, inputs)
-        exchange(c, target, slot)
+        copies = sends(slot)
+        start(copies)
 
         rank = g_query.shape[1]
         up_q = dot(low_t, ctx[...])[:rank]
@@ -412,57 +431,61 @@
             value = dot(d_low_t, nrm[:, at])
             gd[:, at] = value if first else gd[:, at] + value
 
-        return functools.partial(loop, f_pieces, downs)
+        loop(f_pieces, downs)
+        merge(c, target, slot, copies)
 
     x0_local.wait()
     wait(x0_gather)
-    forward(x0, fids, sections - 1 - s, res.at[0], 0, True)
+    forward(x0, fids, sections - 1 - s, res.at[0], 0, True, lambda: None)
 
     @pl.when(s < sections - 1)
     def _():
         forth_hop.start()
 
-    p0_hop.wait()
-    p1_hop.start()
-    s0_hop.start()
-    start(p0_gather)
+    def stored_first():
+        p0_hop.wait()
+        p1_hop.start()
+        start(p0_gather)
+
+    def next_input():
+        @pl.when(s > 0)
+        def _():
+            forth_hop.wait_recv()
+
+        @pl.when(s == 0)
+        def _():
+            x1_local.wait()
+
+        start(x1_gather)
+        s0_hop.start()
+
     c0_local.wait()
     wait(c0_gather)
-    wait(p0_gather)
-
-    backward(p0, c0, bids, s, res.at[1], 2, True)()
+    backward(p0, c0, bids, s, res.at[1], 2, True, stored_first, next_input)
 
     @pl.when(s > 0)
     def _():
         back_hop.start()
-        forth_hop.wait_recv()
-
-    @pl.when(s == 0)
-    def _():
-        x1_local.wait()
-
-    start(x1_gather)
-    s1_hop.start()
+
+    def next_cotangent():
+        @pl.when(s < sections - 1)
+        def _():
+            back_hop.wait_recv()
+
+        @pl.when(s == sections - 1)
+        def _():
+            c1_local.wait()
+
+        start(c1_gather)
+        p1_hop.wait()
+        start(p1_gather)
+        s1_hop.start()
+
     wait(x1_gather)
-
-    forward(x1, fids, sections - s, departing.at[0], 1, False)
-
-    p1_hop.wait()
-    start(p1_gather)
-
-    @pl.when(s < sections - 1)
-    def _():
-        back_hop.wait_recv()
-
-    @pl.when(s == sections - 1)
-    def _():
-        c1_local.wait()
-
-    start(c1_gather)
-    wait(p1_gather)
+    forward(x1, fids, sections - s, departing.at[0], 1, False, next_cotangent)
+
     wait(c1_gather)
-
-    backward(p1, c1, bids, s + 1, returned.at[0], 3, False)()
+    backward(p1, c1, bids, s + 1, returned.at[0], 3, False, lambda: None, lambda: None)
 
     gd_send[...] = gd[...].astype(bf16)
     copies = [
@@ -497,6 +520,17 @@
     s1_hop.wait()
 
 
+def hand_on(count, *refs):
+    sems = refs[2 * count]
+    copies = [
+        pltpu.make_async_copy(refs[i], refs[count + i], sems.at[i]) for i in range(count)
+    ]
+    for copy in copies:
+        copy.start()
+    for copy in copies:
+        copy.wait()
+
+
 def per_device(
     gain, wq, wk, wv, wo, down, qup, vup, arriving, entering, returning, head_grad, parked,
     fids, bids,
@@ -508,16 +542,13 @@
     dq_width, kv_width = wq.shape[2], wk.shape[2]
     rank = qup.shape[1]
     cosines, sines = rope_tables(rows)
-    zeros_q, zeros_v = jnp.zeros_like(qup[0]), jnp.zeros_like(vup[0])
-    qup_wide = jnp.concatenate([qup[0], zeros_q], axis=0)
-    vup_wide = jnp.concatenate([zeros_v, vup[0]], axis=0)
     down_flat = down.reshape(2 * rank, width)
     vmem = pl.BlockSpec(memory_space=pltpu.VMEM)
     anywhere = pl.BlockSpec(memory_space=pl.ANY)
     others = max(shares - 1, 1)
-    pieces = 2 + dq_width // min(512, dq_width) + width // min(512, width)
+    pieces = 2 + dq_width // min(512, dq_width) + width // min(512, share)
     act = pltpu.VMEM((rows, width), bf16)
-    return pl.pallas_call(
+    outs = pl.pallas_call(
         functools.partial(kernel, sections, shares),
         out_shape=(
             jax.ShapeDtypeStruct((1, rows, share), bf16),
@@ -552,6 +583,8 @@
             pltpu.VMEM((2 * rank, width), bf16),
             pltpu.VMEM((others, 2 * rank, share), bf16),
             pltpu.VMEM((rows, rows), jnp.int32),
+            pltpu.VMEM((2 * rank, dq_width), bf16),
+            pltpu.VMEM((2 * rank, kv_width), bf16),
             pltpu.SemaphoreType.DMA((pieces,)),
             pltpu.SemaphoreType.DMA((4,)),
             pltpu.SemaphoreType.DMA((7, others)),
@@ -565,9 +598,16 @@
             collective_id=0, has_side_effects=True, vmem_limit_bytes=63 * 2**20
         ),
     )(
-        gain, down_flat, qup_wide, vup_wide, jnp.asarray(cosines), jnp.asarray(sines),
+        gain, down_flat, qup, vup, jnp.asarray(cosines), jnp.asarray(sines),
         fids, bids, wq, wk, wv, wo, arriving, entering, returning, head_grad, parked,
     )
+    return pl.pallas_call(
+        functools.partial(hand_on, len(outs)),
+        out_shape=tuple(jax.ShapeDtypeStruct(o.shape, o.dtype) for o in outs),
+        in_specs=[anywhere] * len(outs),
+        out_specs=(anywhere,) * len(outs),
+        scratch_shapes=[pltpu.SemaphoreType.DMA((len(outs),))],
+    )(*outs)
 
 
 def solution(mesh):

time: 148 us -> 210 us (1.42)
  Pallas kernels: 134 us -> 209 us
  local copies, waits for them, and re-layouts: 13.1 us -> 0 us
    pallas_call x0 -> x1, Pallas kernels: none -> 71.1 us  [per_device(): pl.pallas_call(functools.partial(hand_on, len(outs)), out_shape=tuple((ja...]
    unnamed x6 -> x0, local copies, waits for them, and re-layouts: 10.4 us -> none
    pallas_call x1, Pallas kernels: 134 us -> 137 us  [per_device(): pl.pallas_call(functools.partial(kernel, sections, shares), out_shape=(ja...]
    concatenate x2 -> x0, local copies, waits for them, and re-layouts: 2.7 us -> none  [the longest x1 1.39 us: per_device(): qup_wide = jnp.concatenate([qup[0], zeros_q], axis=0)]
where the time goes in v2:
time: 210 us; the launch traced here: 209 us
  Pallas kernels  209 us (100%)
    pallas_call x1, Pallas kernels, per_device(): pl.pallas_call(functools.partial(kernel, sections, shares), out_shape=(ja...  137 us
    pallas_call x1, Pallas kernels, per_device(): pl.pallas_call(functools.partial(hand_on, len(outs)), out_shape=tuple((ja...  71.1 us

profile of v2, /device:TPU:15, one launch (start us, length us, event | category | flops | bytes accessed | tf_op | source)
XLA Modules:
  0.0 209.4 jit_solution(4178785643506968344)
XLA Ops:
  0.6 137.4 %shard_map.208 = (bf16[1,128,2048]{2,1,0:T(8,128)(2,1)}, bf16[1,128,2048]{2,1,0:T(8,128)(2,1)}, bf16[1,2,128,2048]{3,2,1,0:T(8,128)(2,1)}, f32[1,2,8,2048]{3,2,1...) custom-call(f32[1,4096]{1,0:T(1,128)} %gain.1, bf16[16,4096]{1,0:T(8,128)(2,1)} %bitcast.1, ...), custom_call_target="tpu_custom_call" | custom-call | tf_op jit(solution)/shard_map/pallas_call | solution.py:551
  138.1 71.1 %shard_map.209 = (bf16[1,128,2048]{2,1,0:T(8,128)(2,1)}, bf16[1,128,2048]{2,1,0:T(8,128)(2,1)}, bf16[1,2,128,2048]{3,2,1,0:T(8,128)(2,1)}, f32[1,2,8,2048]{3,2,1...) custom-call(bf16[1,128,2048]{2,1,0:T(8,128)(2,1)} %get-tuple-element.12.refs_0_, ...), custom_call_target="tpu_custom_call" | custom-call | tf_op jit(solution)/shard_map/pallas_call | solution.py:604
